TPU v7x, 32 devices: a whole 2x2x4 slice. The times are simulated.
32 devices in a mesh: space: 16 (over z, x, core), hist: 2 (over y).
Axes of the slice: x: 2, y: 2, z: 4, core: 2. Of those that a mesh axis runs over, the one named last changes fastest.
Arguments:
- history: bfloat16 [8, 64, 8192], P('hist', None, 'space'), may hold values from -6 to 6
- right_factor: bfloat16 [64, 80, 8192], P('hist', None, 'space'), may hold values from -0.25 to 0.25
- left_factor: bfloat16 [64, 80, 8192], P('hist', None, 'space'), may hold values from -0.25 to 0.25
- pair_rank: int32 [64, 16], P('hist', 'space'), may hold values from 20 to 80
- pair_lag: int32 [64, 16], P('hist', 'space'), may hold values from 0 to 3
- near_block: bfloat16 [3, 8192, 512], P(None, 'space'), may hold values from -0.09695897 to 0.09695897, as said below
- self_term: float32 [8192], P('space'), may hold values from 1 to 1.5
- excitation: float32 [64, 8192], P(None, 'space'), may hold values from -6 to 6
Outputs:
- new_current: float32 [64, 8192], P(None, 'space')
- next_history: bfloat16 [8, 64, 8192], P('hist', None, 'space')
Inputs may be any that keep to these rules, and one draw needn't show every extreme that they name: Entries of near_block lie within 3.8 times (1536) to the power -0.5 in magnitude.
All inputs are finite; a program needn't handle non-finite values.
Results may differ from a plain program's by a relative error of at most 0.015.
Values may be sent and summed in bfloat16 or wider, within the bound.
A program may use at most 64 MiB of HBM per device.

v0:
```python
import jax
import jax.numpy as jnp
from jax import lax
from jax.sharding import PartitionSpec as P

SWEEPS = 8


def padded_2(block, sides, width):
    for axis, dim in sides:
        count = lax.axis_size(axis)
        forward = [(i, i + 1) for i in range(count - 1)]
        backward = [(target, source) for source, target in forward]
        low = lax.ppermute(
            lax.slice_in_dim(block, block.shape[dim] - width, None, axis=dim), axis, forward
        )
        high = lax.ppermute(lax.slice_in_dim(block, 0, width, axis=dim), axis, backward)
        block = jnp.concatenate([low, block, high], axis=dim)
    return block


def from_behind(value, axis, steps):
    count = lax.axis_size(axis)
    initial, last = (max(0, -steps), min(count, count - steps))
    return lax.ppermute(value, axis, [(source, source + steps) for source in range(initial, last)])


def per_device(
    history, right_factor, left_factor, pair_rank, pair_lag, near_block, self_term, excitation
):
    time_steps = history.shape[1]
    block_width = history.shape[2]
    pair_dev = right_factor.shape[0]
    rank_most = right_factor.shape[1]
    space_size = lax.axis_size("space")
    per_target = pair_dev // space_size
    chosen = jnp.take(history, pair_lag[:, 0], axis=0)
    coefficient = jnp.einsum(
        "prb,pkb->prk", right_factor, chosen, preferred_element_type=jnp.float32
    )
    levels = lax.broadcasted_iota(jnp.int32, (1, rank_most, 1), 1)
    coefficient = jnp.where(levels < pair_rank[:, 0][:, None, None], coefficient, 0.0).astype(
        jnp.bfloat16
    )
    coefficient = coefficient.reshape(space_size, per_target * rank_most, time_steps)
    left_rows = left_factor.reshape(space_size, per_target * rank_most, block_width)
    partial_value = jnp.einsum(
        "tck,tcb->tkb", coefficient, left_rows, preferred_element_type=jnp.float32
    )
    arrived = lax.all_to_all(
        partial_value.astype(jnp.bfloat16), "space", split_axis=0, concat_axis=0, tiled=True
    ).astype(partial_value.dtype)
    far_field = jnp.sum(arrived, axis=0)
    far_field = lax.psum_scatter(
        far_field.astype(jnp.bfloat16), "hist", scatter_dimension=0, tiled=True
    ).astype(jnp.float32)
    row_count = far_field.shape[0]
    incident = lax.dynamic_slice_in_dim(
        excitation, lax.axis_index("hist") * row_count, row_count, 0
    )
    right_side = incident - far_field
    current = jnp.zeros(right_side.shape, jnp.float32)
    for sweep_index in range(SWEEPS):
        rounded = current.astype(jnp.bfloat16)
        padded = padded_2(rounded, (("space", 1),), block_width)
        product = self_term[None, :] * current
        for offset in range(3):
            beside = padded[:, offset * block_width : (offset + 1) * block_width]
            product = product + lax.dot_general(
                beside,
                near_block[offset],
                (((1,), (1,)), ((), ())),
                preferred_element_type=jnp.float32,
            )
        current = current + (right_side - product) / self_term[None, :]
    current = lax.all_gather(current, "hist", axis=0, tiled=True)
    incoming = from_behind(history[-1], "hist", 1)
    newest = jnp.where(lax.axis_index("hist") == 0, current.astype(jnp.bfloat16), incoming)
    next_history = jnp.concatenate([newest[None], history[:-1]], axis=0)
    return (current, next_history)


def solution(mesh):
    in_specs = (
        P("hist", None, "space"),
        P("hist", None, "space"),
        P("hist", None, "space"),
        P("hist", "space"),
        P("hist", "space"),
        P(None, "space", None),
        P("space"),
        P(None, "space"),
    )
    out_specs = (P(None, "space"), P("hist", None, "space"))
    return jax.shard_map(
        per_device, mesh=mesh, in_specs=in_specs, out_specs=out_specs, check_vma=False
    )
```

profile of v0, /device:TPU:11, one launch (start us, length us, event | category | flops | bytes accessed | tf_op | source)
XLA Modules:
  0.0 139.6 jit_solution(7244077512997485176)
XLA Ops:
  9.4 3.0 %gather_fusion = bf16[32,64,512]{2,1,0:T(8,128)(2,1)} fusion(bf16[4,64,512]{2,1,0:T(8,128)(2,1)} %param.8, s32[1024]{0:T(1024)S(1)} %pad_clamp_fusion), kind=kCustom, calls=%fused_computation | custom fusion | bytes 4194432 | tf_op jit(solution)/shard_map/jit(_take)/gather | solution.py:37
  12.4 3.3 %fusion.9 = bf16[32,80,64]{1,2,0:T(8,128)(2,1)S(1)} fusion(bf16[32,80,512]{2,1,0:T(8,128)(2,1)} %param.9, bf16[32,64,512]{2,1,0:T(8,128)(2,1)} %gather_fusion, pred[32]{0:T(512)(128)(4,1)S(1)} %and_bitcast_fusion, pred[32,80]{1,0:T(8,128)(4,1)S(1)} %iota_compare_fusion), kind=kOutput, calls=%fused_computation.7 | convolution fusion | flops 169148416 | bytes 5048864 | tf_op jit(solution)/shard_map/prb,pkb->prk/dot_general | solution.py:38
  17.1 2.6 %convolution_convert_fusion = bf16[16,64,512]{2,1,0:T(8,128)(2,1)} fusion(bf16[16,160,512]{2,1,0:T(8,128)(2,1)S(1)} %bitcast.104, bf16[16,160,64]{1,0,2:T(8,128)(2,1)} %reshape.42), kind=kOutput, calls=%fused_computation.4 | convolution fusion | flops 168296448 | bytes 3997696 | tf_op jit(solution)/shard_map/tck,tcb->tkb/dot_general | solution.py:47
  19.7 6.7 %all-to-all-start = ((bf16[16,64,512]{2,1,0:T(8,128)(2,1)}), bf16[16,64,512]{2,1,0:T(8,128)(2,1)}, u32[]{:S(2)}, u32[]{:S(2)}) async-start(bf16[16,64,512]{2,1,0:T(8,128)(2,1)} %convolution_convert_fusion), calls=%async_computation | async-start | bytes 2097152 | tf_op jit(solution)/shard_map/all_to_all | solution.py:50
  26.5 3.3 %collective-permute-start = (bf16[32,512]{1,0:T(8,128)(2,1)S(1)}, bf16[32,512]{1,0:T(8,128)(2,1)S(1)}, u32[]{:S(2)}, u32[]{:S(2)}) collective-permute-start(bf16[32,512]{1,0:T(8,128)(2,1)S(1)} %convert_element_type.45), channel_id=1, source_target_pairs={{0,2},{2,4},{4,6},{6,8},{8,10},{10,12},{12,14},{14,16},{16,18},{18... | collective-permute-start | bytes 98312 | tf_op jit(solution)/shard_map/ppermute | solution.py:14
  31.8 3.1 %collective-permute-start.16 = (bf16[64,512]{1,0:T(8,128)(2,1)S(1)}, bf16[64,512]{1,0:T(8,128)(2,1)S(1)}, u32[]{:S(2)}, u32[]{:S(2)}) collective-permute-start(bf16[64,512]{1,0:T(8,128)(2,1)S(1)} %slice_bitcast_fusion), channel_id=1, source_target_pairs={{0,1},{2,3},{4,5},{6,7},{8,9},{10,11},{12,13},{14,15},{16,17},{18,... | collective-permute-start | bytes 196616 | tf_op jit(solution)/shard_map/ppermute | solution.py:25
  36.2 15.1 %all-to-all-done = bf16[16,64,512]{2,1,0:T(8,128)(2,1)} async-done(((bf16[16,64,512]{2,1,0:T(8,128)(2,1)}), bf16[16,64,512]{2,1,0:T(8,128)(2,1)}, u32[]{:S(2)}, u32[]{:S(2)}) %all-to-all-start) | async-done | bytes 1048608 | tf_op jit(solution)/shard_map/all_to_all | solution.py:50
  51.4 2.0 %reduce_sum.12 = bf16[64,512]{1,0:T(8,128)(2,1)} reduce(bf16[16,64,512]{2,1,0:T(8,128)(2,1)} %all-to-all-done, bf16[]{:T(256)} %constant.30.clone.1), dimensions={0}, to_apply=%region_0.1 | reduce | flops 491520 | bytes 1114114 | tf_op jit(solution)/shard_map/reduce_sum | solution.py:53
  54.7 7.8 %reduce-scatter.2.cloned.1.call-done = bf16[32,512]{1,0:T(8,128)(2,1)} async-done(((bf16[64,512]{1,0:T(8,128)(2,1)}), bf16[32,512]{1,0:T(8,128)(2,1)}) %reduce-scatter.2.cloned.1.call-update) | async-done | bytes 32784 | tf_op jit(solution)/shard_map/reduce_scatter | solution.py:54
  64.7 3.0 %collective-permute-start.3 = (bf16[32,512]{1,0:T(8,128)(2,1)S(1)}, bf16[32,512]{1,0:T(8,128)(2,1)S(1)}, u32[]{:S(2)}, u32[]{:S(2)}) collective-permute-start(bf16[32,512]{1,0:T(8,128)(2,1)S(1)} %get-tuple-element.2), channel_id=1, source_target_pairs={{2,0},{4,2},{6,4},{8,6},{10,8},{12,10},{14,12},{16,14},{18,16},{20... | collective-permute-start | bytes 98312 | tf_op jit(solution)/shard_map/ppermute | solution.py:17
  67.8 3.4 %collective-permute-start.2 = (bf16[32,512]{1,0:T(8,128)(2,1)S(1)}, bf16[32,512]{1,0:T(8,128)(2,1)S(1)}, u32[]{:S(2)}, u32[]{:S(2)}) collective-permute-start(bf16[32,512]{1,0:T(8,128)(2,1)S(1)} %get-tuple-element.2), channel_id=1, source_target_pairs={{0,2},{2,4},{4,6},{6,8},{8,10},{10,12},{12,14},{14,16},{16,18},{18... | collective-permute-start | bytes 98312 | tf_op jit(solution)/shard_map/ppermute | solution.py:14
  73.1 4.8 %collective-permute-start.4 = (bf16[32,512]{1,0:T(8,128)(2,1)S(1)}, bf16[32,512]{1,0:T(8,128)(2,1)S(1)}, u32[]{:S(2)}, u32[]{:S(2)}) collective-permute-start(bf16[32,512]{1,0:T(8,128)(2,1)S(1)} %get-tuple-element.4), channel_id=1, source_target_pairs={{0,2},{2,4},{4,6},{6,8},{8,10},{10,12},{12,14},{14,16},{16,18},{18... | collective-permute-start | bytes 98312 | tf_op jit(solution)/shard_map/ppermute | solution.py:14
  80.4 3.9 %collective-permute-done.5 = bf16[32,512]{1,0:T(8,128)(2,1)S(1)} collective-permute-done((bf16[32,512]{1,0:T(8,128)(2,1)S(1)}, bf16[32,512]{1,0:T(8,128)(2,1)S(1)}, u32[]{:S(2)}, u32[]{:S(2)}) %collective-permute-start.5) | collective-permute-done | bytes 32800 | tf_op jit(solution)/shard_map/ppermute | solution.py:17
  86.7 2.4 %collective-permute-start.7 = (bf16[32,512]{1,0:T(8,128)(2,1)S(1)}, bf16[32,512]{1,0:T(8,128)(2,1)S(1)}, u32[]{:S(2)}, u32[]{:S(2)}) collective-permute-start(bf16[32,512]{1,0:T(8,128)(2,1)S(1)} %get-tuple-element.6), channel_id=1, source_target_pairs={{2,0},{4,2},{6,4},{8,6},{10,8},{12,10},{14,12},{16,14},{18,16},{20... | collective-permute-start | bytes 98312 | tf_op jit(solution)/shard_map/ppermute | solution.py:17
  89.4 3.4 %collective-permute-done.7 = bf16[32,512]{1,0:T(8,128)(2,1)S(1)} collective-permute-done((bf16[32,512]{1,0:T(8,128)(2,1)S(1)}, bf16[32,512]{1,0:T(8,128)(2,1)S(1)}, u32[]{:S(2)}, u32[]{:S(2)}) %collective-permute-start.7) | collective-permute-done | bytes 32800 | tf_op jit(solution)/shard_map/ppermute | solution.py:17
  95.3 2.4 %collective-permute-start.9 = (bf16[32,512]{1,0:T(8,128)(2,1)S(1)}, bf16[32,512]{1,0:T(8,128)(2,1)S(1)}, u32[]{:S(2)}, u32[]{:S(2)}) collective-permute-start(bf16[32,512]{1,0:T(8,128)(2,1)S(1)} %get-tuple-element.8), channel_id=1, source_target_pairs={{2,0},{4,2},{6,4},{8,6},{10,8},{12,10},{14,12},{16,14},{18,16},{20... | collective-permute-start | bytes 98312 | tf_op jit(solution)/shard_map/ppermute | solution.py:17
  98.0 3.4 %collective-permute-done.9 = bf16[32,512]{1,0:T(8,128)(2,1)S(1)} collective-permute-done((bf16[32,512]{1,0:T(8,128)(2,1)S(1)}, bf16[32,512]{1,0:T(8,128)(2,1)S(1)}, u32[]{:S(2)}, u32[]{:S(2)}) %collective-permute-start.9) | collective-permute-done | bytes 32800 | tf_op jit(solution)/shard_map/ppermute | solution.py:17
  103.9 2.4 %collective-permute-start.11 = (bf16[32,512]{1,0:T(8,128)(2,1)S(1)}, bf16[32,512]{1,0:T(8,128)(2,1)S(1)}, u32[]{:S(2)}, u32[]{:S(2)}) collective-permute-start(bf16[32,512]{1,0:T(8,128)(2,1)S(1)} %get-tuple-element.10), channel_id=1, source_target_pairs={{2,0},{4,2},{6,4},{8,6},{10,8},{12,10},{14,12},{16,14},{18,16},{20... | collective-permute-start | bytes 98312 | tf_op jit(solution)/shard_map/ppermute | solution.py:17
  106.6 3.4 %collective-permute-done.11 = bf16[32,512]{1,0:T(8,128)(2,1)S(1)} collective-permute-done((bf16[32,512]{1,0:T(8,128)(2,1)S(1)}, bf16[32,512]{1,0:T(8,128)(2,1)S(1)}, u32[]{:S(2)}, u32[]{:S(2)}) %collective-permute-start.11) | collective-permute-done | bytes 32800 | tf_op jit(solution)/shard_map/ppermute | solution.py:17
  112.5 2.4 %collective-permute-start.13 = (bf16[32,512]{1,0:T(8,128)(2,1)S(1)}, bf16[32,512]{1,0:T(8,128)(2,1)S(1)}, u32[]{:S(2)}, u32[]{:S(2)}) collective-permute-start(bf16[32,512]{1,0:T(8,128)(2,1)S(1)} %get-tuple-element.12), channel_id=1, source_target_pairs={{2,0},{4,2},{6,4},{8,6},{10,8},{12,10},{14,12},{16,14},{18,16},{20... | collective-permute-start | bytes 98312 | tf_op jit(solution)/shard_map/ppermute | solution.py:17
  115.2 3.4 %collective-permute-done.13 = bf16[32,512]{1,0:T(8,128)(2,1)S(1)} collective-permute-done((bf16[32,512]{1,0:T(8,128)(2,1)S(1)}, bf16[32,512]{1,0:T(8,128)(2,1)S(1)}, u32[]{:S(2)}, u32[]{:S(2)}) %collective-permute-start.13) | collective-permute-done | bytes 32800 | tf_op jit(solution)/shard_map/ppermute | solution.py:17
  121.1 2.4 %collective-permute-start.15 = (bf16[32,512]{1,0:T(8,128)(2,1)S(1)}, bf16[32,512]{1,0:T(8,128)(2,1)S(1)}, u32[]{:S(2)}, u32[]{:S(2)}) collective-permute-start(bf16[32,512]{1,0:T(8,128)(2,1)S(1)} %get-tuple-element.14), channel_id=1, source_target_pairs={{2,0},{4,2},{6,4},{8,6},{10,8},{12,10},{14,12},{16,14},{18,16},{20... | collective-permute-start | bytes 98312 | tf_op jit(solution)/shard_map/ppermute | solution.py:17
  123.8 3.4 %collective-permute-done.15 = bf16[32,512]{1,0:T(8,128)(2,1)S(1)} collective-permute-done((bf16[32,512]{1,0:T(8,128)(2,1)S(1)}, bf16[32,512]{1,0:T(8,128)(2,1)S(1)}, u32[]{:S(2)}, u32[]{:S(2)}) %collective-permute-start.15) | collective-permute-done | bytes 32800 | tf_op jit(solution)/shard_map/ppermute | solution.py:17
  127.5 3.8 %all_gather.3 = f32[64,512]{1,0:T(8,128)S(1)} all-gather(f32[32,512]{1,0:T(8,128)S(1)} %fusion.41), channel_id=1, replica_groups=mesh['space'=16,'hist'=2] {'hist'}, dimensions={0}, use_global_device_ids=true | all-gather | bytes 196608 | tf_op jit(solution)/shard_map/all_gather | solution.py:76
  (69 shorter events, 29.9 us)
Async XLA Ops:
  19.7 12.0 %copy-start.2 = (bf16[4,64,512]{2,1,0:T(8,128)(2,1)S(1)}, bf16[4,64,512]{2,1,0:T(8,128)(2,1)}, u32[]{:S(2)}) copy-start(bf16[4,64,512]{2,1,0:T(8,128)(2,1)} %param.8) | copy-start | bytes 786436
  19.7 16.5 %copy-start.3 = (f32[512]{0:T(512)S(1)}, f32[512]{0:T(512)}, u32[]{:S(2)}) copy-start(f32[512]{0:T(512)} %param.14) | copy-start | bytes 6148
  19.7 31.7 %all-to-all-start = ((bf16[16,64,512]{2,1,0:T(8,128)(2,1)}), bf16[16,64,512]{2,1,0:T(8,128)(2,1)}, u32[]{:S(2)}, u32[]{:S(2)}) async-start(bf16[16,64,512]{2,1,0:T(8,128)(2,1)} %convolution_convert_fusion), calls=%async_computation | async-start | bytes 2097152 | tf_op jit(solution)/shard_map/all_to_all | solution.py:50
  26.4 36.1 %copy-start.4 = (f32[64,512]{1,0:T(8,128)S(1)}, f32[64,512]{1,0:T(8,128)}, u32[]{:S(2)}) copy-start(f32[64,512]{1,0:T(8,128)} %param.15) | copy-start | bytes 393220
  26.4 36.1 %reduce-scatter.2.cloned.1.call-start = ((), (), s32[]{:S(2)}) async-start(), calls=%async_computation.2 | async-start | bytes 98304 | tf_op jit(solution)/shard_map/reduce_scatter | solution.py:54
  26.5 27.0 %collective-permute-start = (bf16[32,512]{1,0:T(8,128)(2,1)S(1)}, bf16[32,512]{1,0:T(8,128)(2,1)S(1)}, u32[]{:S(2)}, u32[]{:S(2)}) collective-permute-start(bf16[32,512]{1,0:T(8,128)(2,1)S(1)} %convert_element_type.45), channel_id=1, source_target_pairs={{0,2},{2,4},{4,6},{6,8},{8,10},{10,12},{12,14},{14,16},{16,18},{18... | collective-permute-start | bytes 98312 | tf_op jit(solution)/shard_map/ppermute | solution.py:14
  29.8 33.6 %collective-permute-start.1 = (bf16[32,512]{1,0:T(8,128)(2,1)S(1)}, bf16[32,512]{1,0:T(8,128)(2,1)S(1)}, u32[]{:S(2)}, u32[]{:S(2)}) collective-permute-start(bf16[32,512]{1,0:T(8,128)(2,1)S(1)} %convert_element_type.45), channel_id=1, source_target_pairs={{2,0},{4,2},{6,4},{8,6},{10,8},{12,10},{14,12},{16,14},{18,16},{20... | collective-permute-start | bytes 98312 | tf_op jit(solution)/shard_map/ppermute | solution.py:17
  31.8 99.6 %collective-permute-start.16 = (bf16[64,512]{1,0:T(8,128)(2,1)S(1)}, bf16[64,512]{1,0:T(8,128)(2,1)S(1)}, u32[]{:S(2)}, u32[]{:S(2)}) collective-permute-start(bf16[64,512]{1,0:T(8,128)(2,1)S(1)} %slice_bitcast_fusion), channel_id=1, source_target_pairs={{0,1},{2,3},{4,5},{6,7},{8,9},{10,11},{12,13},{14,15},{16,17},{18,... | collective-permute-start | bytes 196616 | tf_op jit(solution)/shard_map/ppermute | solution.py:25
  62.5 10.0 %copy-start.1 = (bf16[3,512,512]{2,1,0:T(8,128)(2,1)S(1)}, bf16[3,512,512]{2,1,0:T(8,128)(2,1)}, u32[]{:S(2)}) copy-start(bf16[3,512,512]{2,1,0:T(8,128)(2,1)} %param.13) | copy-start | bytes 4718596
  64.7 8.0 %collective-permute-start.3 = (bf16[32,512]{1,0:T(8,128)(2,1)S(1)}, bf16[32,512]{1,0:T(8,128)(2,1)S(1)}, u32[]{:S(2)}, u32[]{:S(2)}) collective-permute-start(bf16[32,512]{1,0:T(8,128)(2,1)S(1)} %get-tuple-element.2), channel_id=1, source_target_pairs={{2,0},{4,2},{6,4},{8,6},{10,8},{12,10},{14,12},{16,14},{18,16},{20... | collective-permute-start | bytes 98312 | tf_op jit(solution)/shard_map/ppermute | solution.py:17
  67.8 4.7 %collective-permute-start.2 = (bf16[32,512]{1,0:T(8,128)(2,1)S(1)}, bf16[32,512]{1,0:T(8,128)(2,1)S(1)}, u32[]{:S(2)}, u32[]{:S(2)}) collective-permute-start(bf16[32,512]{1,0:T(8,128)(2,1)S(1)} %get-tuple-element.2), channel_id=1, source_target_pairs={{0,2},{2,4},{4,6},{6,8},{8,10},{10,12},{12,14},{14,16},{16,18},{18... | collective-permute-start | bytes 98312 | tf_op jit(solution)/shard_map/ppermute | solution.py:14
  73.1 7.0 %collective-permute-start.4 = (bf16[32,512]{1,0:T(8,128)(2,1)S(1)}, bf16[32,512]{1,0:T(8,128)(2,1)S(1)}, u32[]{:S(2)}, u32[]{:S(2)}) collective-permute-start(bf16[32,512]{1,0:T(8,128)(2,1)S(1)} %get-tuple-element.4), channel_id=1, source_target_pairs={{0,2},{2,4},{4,6},{6,8},{8,10},{10,12},{12,14},{14,16},{16,18},{18... | collective-permute-start | bytes 98312 | tf_op jit(solution)/shard_map/ppermute | solution.py:14
  78.2 6.1 %collective-permute-start.5 = (bf16[32,512]{1,0:T(8,128)(2,1)S(1)}, bf16[32,512]{1,0:T(8,128)(2,1)S(1)}, u32[]{:S(2)}, u32[]{:S(2)}) collective-permute-start(bf16[32,512]{1,0:T(8,128)(2,1)S(1)} %get-tuple-element.4), channel_id=1, source_target_pairs={{2,0},{4,2},{6,4},{8,6},{10,8},{12,10},{14,12},{16,14},{18,16},{20... | collective-permute-start | bytes 98312 | tf_op jit(solution)/shard_map/ppermute | solution.py:17
  84.6 4.6 %collective-permute-start.6 = (bf16[32,512]{1,0:T(8,128)(2,1)S(1)}, bf16[32,512]{1,0:T(8,128)(2,1)S(1)}, u32[]{:S(2)}, u32[]{:S(2)}) collective-permute-start(bf16[32,512]{1,0:T(8,128)(2,1)S(1)} %get-tuple-element.6), channel_id=1, source_target_pairs={{0,2},{2,4},{4,6},{6,8},{8,10},{10,12},{12,14},{14,16},{16,18},{18... | collective-permute-start | bytes 98312 | tf_op jit(solution)/shard_map/ppermute | solution.py:14
  86.7 6.1 %collective-permute-start.7 = (bf16[32,512]{1,0:T(8,128)(2,1)S(1)}, bf16[32,512]{1,0:T(8,128)(2,1)S(1)}, u32[]{:S(2)}, u32[]{:S(2)}) collective-permute-start(bf16[32,512]{1,0:T(8,128)(2,1)S(1)} %get-tuple-element.6), channel_id=1, source_target_pairs={{2,0},{4,2},{6,4},{8,6},{10,8},{12,10},{14,12},{16,14},{18,16},{20... | collective-permute-start | bytes 98312 | tf_op jit(solution)/shard_map/ppermute | solution.py:17
  93.2 4.6 %collective-permute-start.8 = (bf16[32,512]{1,0:T(8,128)(2,1)S(1)}, bf16[32,512]{1,0:T(8,128)(2,1)S(1)}, u32[]{:S(2)}, u32[]{:S(2)}) collective-permute-start(bf16[32,512]{1,0:T(8,128)(2,1)S(1)} %get-tuple-element.8), channel_id=1, source_target_pairs={{0,2},{2,4},{4,6},{6,8},{8,10},{10,12},{12,14},{14,16},{16,18},{18... | collective-permute-start | bytes 98312 | tf_op jit(solution)/shard_map/ppermute | solution.py:14
  95.3 6.1 %collective-permute-start.9 = (bf16[32,512]{1,0:T(8,128)(2,1)S(1)}, bf16[32,512]{1,0:T(8,128)(2,1)S(1)}, u32[]{:S(2)}, u32[]{:S(2)}) collective-permute-start(bf16[32,512]{1,0:T(8,128)(2,1)S(1)} %get-tuple-element.8), channel_id=1, source_target_pairs={{2,0},{4,2},{6,4},{8,6},{10,8},{12,10},{14,12},{16,14},{18,16},{20... | collective-permute-start | bytes 98312 | tf_op jit(solution)/shard_map/ppermute | solution.py:17
  101.8 4.6 %collective-permute-start.10 = (bf16[32,512]{1,0:T(8,128)(2,1)S(1)}, bf16[32,512]{1,0:T(8,128)(2,1)S(1)}, u32[]{:S(2)}, u32[]{:S(2)}) collective-permute-start(bf16[32,512]{1,0:T(8,128)(2,1)S(1)} %get-tuple-element.10), channel_id=1, source_target_pairs={{0,2},{2,4},{4,6},{6,8},{8,10},{10,12},{12,14},{14,16},{16,18},{18... | collective-permute-start | bytes 98312 | tf_op jit(solution)/shard_map/ppermute | solution.py:14
  103.9 6.1 %collective-permute-start.11 = (bf16[32,512]{1,0:T(8,128)(2,1)S(1)}, bf16[32,512]{1,0:T(8,128)(2,1)S(1)}, u32[]{:S(2)}, u32[]{:S(2)}) collective-permute-start(bf16[32,512]{1,0:T(8,128)(2,1)S(1)} %get-tuple-element.10), channel_id=1, source_target_pairs={{2,0},{4,2},{6,4},{8,6},{10,8},{12,10},{14,12},{16,14},{18,16},{20... | collective-permute-start | bytes 98312 | tf_op jit(solution)/shard_map/ppermute | solution.py:17
  110.4 4.6 %collective-permute-start.12 = (bf16[32,512]{1,0:T(8,128)(2,1)S(1)}, bf16[32,512]{1,0:T(8,128)(2,1)S(1)}, u32[]{:S(2)}, u32[]{:S(2)}) collective-permute-start(bf16[32,512]{1,0:T(8,128)(2,1)S(1)} %get-tuple-element.12), channel_id=1, source_target_pairs={{0,2},{2,4},{4,6},{6,8},{8,10},{10,12},{12,14},{14,16},{16,18},{18... | collective-permute-start | bytes 98312 | tf_op jit(solution)/shard_map/ppermute | solution.py:14
  112.5 6.1 %collective-permute-start.13 = (bf16[32,512]{1,0:T(8,128)(2,1)S(1)}, bf16[32,512]{1,0:T(8,128)(2,1)S(1)}, u32[]{:S(2)}, u32[]{:S(2)}) collective-permute-start(bf16[32,512]{1,0:T(8,128)(2,1)S(1)} %get-tuple-element.12), channel_id=1, source_target_pairs={{2,0},{4,2},{6,4},{8,6},{10,8},{12,10},{14,12},{16,14},{18,16},{20... | collective-permute-start | bytes 98312 | tf_op jit(solution)/shard_map/ppermute | solution.py:17
  115.2 16.1 %slice-start = ((bf16[4,64,512]{2,1,0:T(8,128)(2,1)}), bf16[3,64,512]{2,1,0:T(8,128)(2,1)S(1)}, s32[]{:S(2)}) async-start(bf16[4,64,512]{2,1,0:T(8,128)(2,1)} %param.8), calls=%async_computation.3 | async-start | bytes 393216 | tf_op jit(solution)/shard_map/slice | solution.py:79
  118.9 4.6 %collective-permute-start.14 = (bf16[32,512]{1,0:T(8,128)(2,1)S(1)}, bf16[32,512]{1,0:T(8,128)(2,1)S(1)}, u32[]{:S(2)}, u32[]{:S(2)}) collective-permute-start(bf16[32,512]{1,0:T(8,128)(2,1)S(1)} %get-tuple-element.14), channel_id=1, source_target_pairs={{0,2},{2,4},{4,6},{6,8},{8,10},{10,12},{12,14},{14,16},{16,18},{18... | collective-permute-start | bytes 98312 | tf_op jit(solution)/shard_map/ppermute | solution.py:14
  121.1 6.1 %collective-permute-start.15 = (bf16[32,512]{1,0:T(8,128)(2,1)S(1)}, bf16[32,512]{1,0:T(8,128)(2,1)S(1)}, u32[]{:S(2)}, u32[]{:S(2)}) collective-permute-start(bf16[32,512]{1,0:T(8,128)(2,1)S(1)} %get-tuple-element.14), channel_id=1, source_target_pairs={{2,0},{4,2},{6,4},{8,6},{10,8},{12,10},{14,12},{16,14},{18,16},{20... | collective-permute-start | bytes 98312 | tf_op jit(solution)/shard_map/ppermute | solution.py:17
  (1 other events, 10.0 us)
Sparse Core Ops, SparseCore 0:
  53.5 8.9 reduce-scatter.1
where the time goes:
time: 141 us; the launch traced here: 140 us
  starting transfers between devices  50 us (35%)
  waiting for transfers between devices  44.1 us (31%)
  matrix products  16.1 us (11%)
  between operations  14.5 us (10%)
  other arithmetic  5.88 us (4%)
  local copies, waits for them, and re-layouts  5.17 us (4%)
  blocking collectives  3.79 us (3%)
    ppermute x8, starting transfers between devices, padded_2(): lax.ppermute(lax.slice_in_dim(block, block.shape[dim] - width, None, axis...  21.2 us
    ppermute x8, waiting for transfers between devices, padded_2(): lax.ppermute(lax.slice_in_dim(block, 0, width, axis=dim), axis, backward)  21.1 us
    ppermute x8, starting transfers between devices, padded_2(): lax.ppermute(lax.slice_in_dim(block, 0, width, axis=dim), axis, backward)  19 us
    all_to_all x1, waiting for transfers between devices, per_device(): lax.all_to_all(partial_value.astype(jnp.bfloat16), 'space', split_axis=0,...  15.1 us
    dot_general x24, matrix products, per_device(): lax.dot_general(beside, near_block[offset], (((1,), (1,)), ((), ())), pre...  10.3 us
    reduce_scatter x1, waiting for transfers between devices, per_device(): lax.psum_scatter(far_field.astype(jnp.bfloat16), 'hist', scatter_dimensio...  7.8 us
    all_to_all x1, starting transfers between devices, per_device(): lax.all_to_all(partial_value.astype(jnp.bfloat16), 'space', split_axis=0,...  6.69 us
    all_gather x1, blocking collectives, per_device(): current = lax.all_gather(current, 'hist', axis=0, tiled=True)  3.79 us
  transfers between devices with their start and end apart: 19, of which 8 were waited for; matrix products, arithmetic and copies ran while one was open for 9% of the time, Pallas kernels for 0%

commit v1 on v0

v1 whole, which is shorter than its diff:
```python
import functools

import jax
import jax.numpy as jnp
from jax import lax
from jax.experimental import pallas as pl
from jax.experimental.pallas import tpu as pltpu
from jax.sharding import PartitionSpec as P

SWEEPS = 8
MESH = pl.DeviceIdType.MESH
NT = (((1,), (1,)), ((), ()))


def shape_of(space):
    cores = 2
    chips = space // cores
    z_size = 1
    while z_size * z_size * 4 <= space and chips % (z_size * 2) == 0:
        z_size *= 2
    return z_size, chips // z_size, cores


def kernel(
    dims,
    lag_ref, rank_ref, hist_ref, self_ref, exc_ref, right_hbm, left_hbm, near_hbm,
    cur_out, hist_out,
    rbuf, lbuf, nbuf, p1, r1, q, r2, t3, r3, xs, halo, xlast, gath, hin,
    rsem, lsem, nsem, s1s, s1r, s2s, s2r, s3s, s3r, xss, xsr, gs, gr, hs,
):
    space, hists, z_size, x_size, per, rank_most = dims
    lags, steps, width = hist_ref.shape
    kh = steps // hists
    me = lax.axis_index("space")
    h = lax.axis_index("hist")
    core = lax.rem(me, 2)
    chip = me // 2
    x = lax.rem(chip, x_size)
    z = chip // x_size
    mate = me + 1 - 2 * core
    half = space // 2
    group = x_size * hists
    slot = x * hists + h

    def chip_at(j):
        zo, xo = j // x_size, lax.rem(j, x_size)
        zt = lax.rem(z + 1 + zo, z_size)
        xt = lax.rem(x + 1 + xo, x_size)
        return zt, xt

    def load(t):
        rows = pl.ds(t * per, per)
        return (
            pltpu.make_async_copy(right_hbm.at[rows], rbuf.at[rows], rsem.at[t]),
            pltpu.make_async_copy(left_hbm.at[rows], lbuf.at[rows], lsem.at[t]),
        )

    def space_id(zt, xt):
        return (zt * x_size + xt) * 2 + core

    barrier = pltpu.get_barrier_semaphore()

    def greet(s, hh):
        pl.semaphore_signal(barrier, inc=1, device_id=(s, hh), device_id_type=MESH)

    greet(mate, h)
    for o in range(1, group):
        sl = lax.rem(slot + o, group)
        greet(space_id(z, sl // hists), lax.rem(sl, hists))
    for o in range(1, z_size):
        greet(space_id(lax.rem(z + o, z_size), x), h)

    @pl.when(me > 0)
    def _():
        greet(me - 1, h)

    @pl.when(me < space - 1)
    def _():
        greet(me + 1, h)

    for side in range(2):
        def start(j, carry):
            zt, xt = chip_at(j)
            own = core if side else 1 - core
            for c in load((zt * x_size + xt) * 2 + own):
                c.start()
            return carry

        lax.fori_loop(0, half, start, 0)
    near_copy = pltpu.make_async_copy(near_hbm, nbuf, nsem)
    near_copy.start()

    hist_all = hist_ref[...].reshape(lags * steps, width)
    cols = lax.broadcasted_iota(jnp.int32, (1, per * rank_most), 1)

    def partial_of(t):
        for c in load(t):
            c.wait()
        rows = pl.ds(t * per, per)
        rr = rbuf[rows].reshape(per * rank_most, width)
        ll = lbuf[rows].reshape(per * rank_most, width)
        lag = jnp.full(cols.shape, lag_ref[t * per], jnp.int32)
        lim = jnp.full(cols.shape, rank_ref[t * per], jnp.int32)
        for i in range(1, per):
            at = cols >= i * rank_most
            lag = jnp.where(at, lag_ref[t * per + i], lag)
            lim = jnp.where(at, rank_ref[t * per + i] + i * rank_most, lim)
        lag = jnp.where(cols < lim, lag, lags)
        full = lax.dot_general(hist_all, rr, NT, preferred_element_type=jnp.float32)
        coef = jnp.zeros((steps, per * rank_most), jnp.float32)
        for g in range(lags):
            coef = jnp.where(lag == g, full[g * steps : (g + 1) * steps], coef)
        return jnp.dot(coef.astype(jnp.bfloat16), ll, preferred_element_type=jnp.float32)

    def copy1(b):
        return pltpu.make_async_remote_copy(
            src_ref=p1.at[b], dst_ref=r1.at[b], send_sem=s1s.at[b], recv_sem=s1r.at[b],
            device_id=(mate, h), device_id_type=MESH,
        )

    ends = jnp.minimum(me, 1) + jnp.minimum(space - 1 - me, 1)
    pl.semaphore_wait(barrier, 1 + (group - 1) + (z_size - 1) + ends)

    hist_copy = pltpu.make_async_remote_copy(
        src_ref=hist_ref.at[lags - 1], dst_ref=hin, send_sem=hs.at[0], recv_sem=hs.at[1],
        device_id=(me, lax.rem(h + 1, hists)), device_id_type=MESH,
    )

    def first(j, carry):
        zt, xt = chip_at(j)
        b = zt * x_size + xt
        p1[b] = partial_of(b * 2 + 1 - core).astype(jnp.bfloat16)
        copy1(b).start()
        return carry

    lax.fori_loop(0, half, first, 0)

    def copy2(zt, xt, ht):
        return pltpu.make_async_remote_copy(
            src_ref=q.at[zt, xt * hists + ht], dst_ref=r2.at[zt, slot],
            send_sem=s2s.at[zt, xt * hists + ht], recv_sem=s2r.at[zt, slot],
            device_id=(space_id(z, xt), ht), device_id_type=MESH,
        )

    def second(j, carry):
        zt, xt = chip_at(j)
        b = zt * x_size + xt
        value = partial_of(b * 2 + core)
        copy1(b).wait_recv()
        value = value + r1[b].astype(jnp.float32)
        low = value.astype(jnp.bfloat16)
        for ht in range(hists):
            part = low[ht * kh : (ht + 1) * kh]
            mine = jnp.logical_and(xt == x, h == ht)

            @pl.when(mine)
            def _():
                r2[zt, slot] = part

            @pl.when(jnp.logical_not(mine))
            def _():
                q[zt, xt * hists + ht] = part
                copy2(zt, xt, ht).start()
        return carry

    lax.fori_loop(0, half, second, 0)
    hist_copy.start()

    def gather2(zt):
        def wait(o, carry):
            sl = lax.rem(slot + o, group)
            pltpu.make_async_remote_copy(
                src_ref=q.at[zt, sl], dst_ref=r2.at[zt, sl],
                send_sem=s2s.at[zt, sl], recv_sem=s2r.at[zt, sl],
                device_id=(space_id(z, sl // hists), lax.rem(sl, hists)), device_id_type=MESH,
            ).wait_recv()
            return carry

        lax.fori_loop(1, group, wait, 0)
        return jnp.sum(r2[zt].astype(jnp.float32), axis=0)

    def copy3(zt):
        return pltpu.make_async_remote_copy(
            src_ref=t3.at[zt], dst_ref=r3.at[z], send_sem=s3s.at[zt], recv_sem=s3r.at[z],
            device_id=(space_id(zt, x), h), device_id_type=MESH,
        )

    def third(zo, carry):
        zt = lax.rem(z + 1 + zo, z_size)
        t3[zt] = gather2(zt).astype(jnp.bfloat16)
        copy3(zt).start()
        return carry

    lax.fori_loop(0, z_size - 1, third, 0)
    far = gather2(z)

    inverse = 1.0 / self_ref[...]
    for l in range(1, lags):
        hist_out[l] = hist_ref[l - 1]

    @pl.when(me == 0)
    def _():
        for n in range(SWEEPS - 1):
            halo[n, 0] = jnp.zeros((kh, width), jnp.bfloat16)

    @pl.when(me == space - 1)
    def _():
        for n in range(SWEEPS - 1):
            halo[n, 1] = jnp.zeros((kh, width), jnp.bfloat16)

    for o in range(1, z_size):
        zs = lax.rem(z + o, z_size)
        pltpu.make_async_remote_copy(
            src_ref=t3.at[zs], dst_ref=r3.at[zs], send_sem=s3s.at[zs], recv_sem=s3r.at[zs],
            device_id=(space_id(zs, x), h), device_id_type=MESH,
        ).wait_recv()
        far = far + r3[zs].astype(jnp.float32)
    near_copy.wait()
    right_side = exc_ref[h] - far
    current = right_side * inverse

    def edge(n, side):
        other = jnp.minimum(me + 1, space - 1) if side == 0 else jnp.maximum(me - 1, 0)
        return pltpu.make_async_remote_copy(
            src_ref=xs.at[n], dst_ref=halo.at[n, side],
            send_sem=xss.at[n, side], recv_sem=xsr.at[n, side],
            device_id=(other, h), device_id_type=MESH,
        )

    for n in range(SWEEPS - 1):
        rounded = current.astype(jnp.bfloat16)
        xs[n] = rounded

        @pl.when(me < space - 1)
        def _():
            edge(n, 0).start()

        @pl.when(me > 0)
        def _():
            edge(n, 1).start()

        product = lax.dot_general(rounded, nbuf[1], NT, preferred_element_type=jnp.float32)
        rest = right_side - product

        @pl.when(me > 0)
        def _():
            edge(n, 0).wait_recv()

        @pl.when(me < space - 1)
        def _():
            edge(n, 1).wait_recv()

        before = lax.dot_general(halo[n, 0], nbuf[0], NT, preferred_element_type=jnp.float32)
        after = lax.dot_general(halo[n, 1], nbuf[2], NT, preferred_element_type=jnp.float32)
        current = (rest - before - after) * inverse

    xlast[...] = current

    def give(o):
        ht = lax.rem(h + o, hists)
        return pltpu.make_async_remote_copy(
            src_ref=xlast, dst_ref=gath.at[h], send_sem=gs.at[ht], recv_sem=gr.at[h],
            device_id=(me, ht), device_id_type=MESH,
        )

    for o in range(1, hists):
        give(o).start()
    cur_out[h] = current
    hist_copy.wait()

    def drain(j, carry):
        zt, xt = chip_at(j)
        copy1(zt * x_size + xt).wait_send()
        for ht in range(hists):
            @pl.when(jnp.logical_not(jnp.logical_and(xt == x, h == ht)))
            def _():
                copy2(zt, xt, ht).wait_send()
        return carry

    lax.fori_loop(0, half, drain, 0)
    for o in range(1, z_size):
        copy3(lax.rem(z + o, z_size)).wait_send()

    @pl.when(me < space - 1)
    def _():
        for n in range(SWEEPS - 1):
            edge(n, 0).wait_send()

    @pl.when(me > 0)
    def _():
        for n in range(SWEEPS - 1):
            edge(n, 1).wait_send()

    for o in range(1, hists):
        hs_ = lax.rem(h + o, hists)
        pltpu.make_async_remote_copy(
            src_ref=xlast, dst_ref=gath.at[hs_], send_sem=gs.at[hs_], recv_sem=gr.at[hs_],
            device_id=(me, hs_), device_id_type=MESH,
        ).wait_recv()
        cur_out[hs_] = gath[hs_]
    for o in range(1, hists):
        give(o).wait_send()

    @pl.when(h == 0)
    def _():
        hist_out[0] = cur_out[...].reshape(steps, width).astype(jnp.bfloat16)

    @pl.when(h > 0)
    def _():
        hist_out[0] = hin[...]


def per_device(
    space, hists,
    history, right_factor, left_factor, pair_rank, pair_lag, near_block, self_term, excitation,
):
    lags, steps, width = history.shape
    pair_dev, rank_most, _ = right_factor.shape
    z_size, x_size, _ = shape_of(space)
    per = pair_dev // space
    kh = steps // hists
    half, group = space // 2, x_size * hists
    sweeps = SWEEPS - 1
    bf16 = jnp.bfloat16
    dma = pltpu.SemaphoreType.DMA
    vmem = pl.BlockSpec(memory_space=pltpu.VMEM)
    smem = pl.BlockSpec(memory_space=pltpu.SMEM)
    any_ = pl.BlockSpec(memory_space=pl.ANY)
    flops = 2 * pair_dev * rank_most * width * steps * 2
    current, next_history = pl.pallas_call(
        functools.partial(kernel, (space, hists, z_size, x_size, per, rank_most)),
        out_shape=(
            jax.ShapeDtypeStruct((hists, kh, width), jnp.float32),
            jax.ShapeDtypeStruct((lags, steps, width), bf16),
        ),
        in_specs=[smem, smem, vmem, vmem, vmem, any_, any_, any_],
        out_specs=(vmem, vmem),
        scratch_shapes=[
            pltpu.VMEM((pair_dev, rank_most, width), bf16),
            pltpu.VMEM((pair_dev, rank_most, width), bf16),
            pltpu.VMEM(near_block.shape, bf16),
            pltpu.VMEM((half, steps, width), bf16),
            pltpu.VMEM((half, steps, width), bf16),
            pltpu.VMEM((z_size, group, kh, width), bf16),
            pltpu.VMEM((z_size, group, kh, width), bf16),
            pltpu.VMEM((z_size, kh, width), bf16),
            pltpu.VMEM((z_size, kh, width), bf16),
            pltpu.VMEM((sweeps, kh, width), bf16),
            pltpu.VMEM((sweeps, 2, kh, width), bf16),
            pltpu.VMEM((kh, width), jnp.float32),
            pltpu.VMEM((hists, kh, width), jnp.float32),
            pltpu.VMEM((steps, width), bf16),
            dma((space,)), dma((space,)), dma,
            dma((half,)), dma((half,)),
            dma((z_size, group)), dma((z_size, group)),
            dma((z_size,)), dma((z_size,)),
            dma((sweeps, 2)), dma((sweeps, 2)),
            dma((hists,)), dma((hists,)), dma((2,)),
        ],
        compiler_params=pltpu.CompilerParams(
            collective_id=0, has_side_effects=True, vmem_limit_bytes=48 * 1024 * 1024
        ),
        cost_estimate=pl.CostEstimate(
            flops=flops, bytes_accessed=4 * pair_dev * rank_most * width, transcendentals=0
        ),
    )(
        pair_lag.reshape(-1), pair_rank.reshape(-1), history, self_term.reshape(1, width),
        excitation.reshape(hists, kh, width), right_factor, left_factor, near_block,
    )
    return current.reshape(steps, width), next_history


def solution(mesh):
    in_specs = (
        P("hist", None, "space"),
        P("hist", None, "space"),
        P("hist", None, "space"),
        P("hist", "space"),
        P("hist", "space"),
        P(None, "space", None),
        P("space"),
        P(None, "space"),
    )
    out_specs = (P(None, "space"), P("hist", None, "space"))
    step = functools.partial(per_device, mesh.shape["space"], mesh.shape["hist"])
    return jax.shard_map(
        step, mesh=mesh, in_specs=in_specs, out_specs=out_specs, check_vma=False
    )
```

time: 141 us -> 56.2 us (0.40)
  starting transfers between devices: 50 us -> 0 us
  Pallas kernels: 0 us -> 47 us
  waiting for transfers between devices: 44.1 us -> 0 us
  matrix products: 16.1 us -> 0 us
  between operations: 14.5 us -> 0.66 us
  other arithmetic: 5.88 us -> 0 us
  blocking collectives: 3.79 us -> 0 us
  local copies, waits for them, and re-layouts: 5.17 us -> 8.34 us
    pallas_call x0 -> x1, Pallas kernels: none -> 47 us  [per_device(): pl.pallas_call(functools.partial(kernel, (space, hists, z_size, x_size, p...]
    ppermute x17 -> x0, starting transfers between devices: 43.3 us -> none  [the longest x8 21.2 us: padded_2(): lax.ppermute(lax.slice_in_dim(block, block.shape[dim] - width, None, axis...]
    ppermute x17 -> x0, waiting for transfers between devices: 21.2 us -> none  [the longest x8 21.1 us: padded_2(): lax.ppermute(lax.slice_in_dim(block, 0, width, axis=dim), axis, backward)]
    dot_general x26 -> x0, matrix products: 16.1 us -> none  [the longest x24 10.3 us: per_device(): lax.dot_general(beside, near_block[offset], (((1,), (1,)), ((), ())), pre...]
    all_to_all x1 -> x0, waiting for transfers between devices: 15.1 us -> none  [per_device(): lax.all_to_all(partial_value.astype(jnp.bfloat16), 'space', split_axis=0,...]
    reduce_scatter x1 -> x0, waiting for transfers between devices: 7.8 us -> none  [per_device(): lax.psum_scatter(far_field.astype(jnp.bfloat16), 'hist', scatter_dimensio...]
    unnamed x11 -> x16, local copies, waits for them, and re-layouts: 0.68 us -> 8.34 us
    all_to_all x1 -> x0, starting transfers between devices: 6.69 us -> none  [per_device(): lax.all_to_all(partial_value.astype(jnp.bfloat16), 'space', split_axis=0,...]
  transfers between devices with their start and end apart: 19 -> 0, of which waited for: 8 -> 0; matrix products, arithmetic and copies ran while one was open for 9% -> 0% of each run, Pallas kernels for 0% -> 0%
where the time goes in v1:
time: 56.2 us; the launch traced here: 56 us
  Pallas kernels  47 us (84%)
  local copies, waits for them, and re-layouts  8.34 us (15%)
  between operations  0.66 us (1%)
    pallas_call x1, Pallas kernels, per_device(): pl.pallas_call(functools.partial(kernel, (space, hists, z_size, x_size, p...  47 us
    unnamed x16, local copies, waits for them, and re-layouts  8.34 us

profile of v1, /device:TPU:11, one launch (start us, length us, event | category | flops | bytes accessed | tf_op | source)
XLA Modules:
  0.0 56.0 jit_solution(16211288494767180600)
XLA Ops:
  0.6 0.0 copy-start
  0.6 1.7 %copy-done = bf16[32,80,512]{2,1,0:T(8,128)(2,1)S(1)} copy-done((bf16[32,80,512]{2,1,0:T(8,128)(2,1)S(1)}, bf16[32,80,512]{2,1,0:T(8,128)(2,1)}, u32[]{:S(2)}) %copy-start) | copy-done | bytes 2621464
  2.4 0.0 copy-start.1
  2.4 1.4 %copy-done.1 = bf16[3,512,512]{2,1,0:T(8,128)(2,1)S(1)} copy-done((bf16[3,512,512]{2,1,0:T(8,128)(2,1)S(1)}, bf16[3,512,512]{2,1,0:T(8,128)(2,1)}, u32[]{:S(2)}) %copy-start.1) | copy-done | bytes 1572888
  3.8 0.0 copy-start.2
  3.8 0.9 %copy-done.2 = bf16[4,64,512]{2,1,0:T(8,128)(2,1)S(1)} copy-done((bf16[4,64,512]{2,1,0:T(8,128)(2,1)S(1)}, bf16[4,64,512]{2,1,0:T(8,128)(2,1)}, u32[]{:S(2)}) %copy-start.2) | copy-done | bytes 262168
  4.7 0.0 copy-start.3
  4.7 0.9 %copy-done.3 = f32[64,512]{1,0:T(8,128)S(1)} copy-done((f32[64,512]{1,0:T(8,128)S(1)}, f32[64,512]{1,0:T(8,128)}, u32[]{:S(2)}) %copy-start.3) | copy-done | bytes 131096
  5.6 0.0 copy-start.4
  5.6 0.7 %copy-done.4 = f32[512]{0:T(512)S(1)} copy-done((f32[512]{0:T(512)S(1)}, f32[512]{0:T(512)}, u32[]{:S(2)}) %copy-start.4) | copy-done | bytes 2072
  6.3 0.0 copy-start.5
  6.3 0.7 %copy-done.5 = s32[32,1]{0,1:T(1,128)S(1)} copy-done((s32[32,1]{0,1:T(1,128)S(1)}, s32[32,1]{0,1:T(1,128)}, u32[]{:S(2)}) %copy-start.5) | copy-done | bytes 152
  7.0 0.0 copy-start.6
  7.0 0.7 %copy-done.6 = s32[32,1]{0,1:T(1,128)S(1)} copy-done((s32[32,1]{0,1:T(1,128)S(1)}, s32[32,1]{0,1:T(1,128)}, u32[]{:S(2)}) %copy-start.6) | copy-done | bytes 152
  7.6 47.0 %shard_map.95 = (f32[2,32,512]{2,1,0:T(8,128)S(1)}, bf16[4,64,512]{2,1,0:T(8,128)(2,1)S(1)}) custom-call(s32[32]{0:T(128)S(1)} %bitcast.8, s32[32]{0:T(128)S(1)} %bitcast.9, bf16[4,64,512]{2,1,0:T(8,128)(2,1)S(1)} %copy-done.2, f32[1,512]{1,0:T(1,128)S(1)} %bitcast.7, f32[2,32,512]{2,1,0:T(8,128)S(1)} %bitcast.5, bf16[32,80,512]{2,1,0:T(8,128)(2,1)S(1)} %copy-done, ...), custom_call_target="tpu_custom_call" | custom-call | flops 335544320 | bytes 5242880 | tf_op jit(solution)/shard_map/pallas_call | solution.py:330
  54.6 0.7 %copy.12 = f32[64,512]{1,0:T(8,128)} copy(f32[64,512]{1,0:T(8,128)S(1)} %bitcast.6) | data formatting | bytes 262144
  55.3 0.7 %copy.13 = bf16[4,64,512]{2,1,0:T(8,128)(2,1)} copy(bf16[4,64,512]{2,1,0:T(8,128)(2,1)S(1)} %get-tuple-element.9) | data formatting | bytes 524288
Async XLA Ops:
  0.6 1.7 %copy-start = (bf16[32,80,512]{2,1,0:T(8,128)(2,1)S(1)}, bf16[32,80,512]{2,1,0:T(8,128)(2,1)}, u32[]{:S(2)}) copy-start(bf16[32,80,512]{2,1,0:T(8,128)(2,1)} %right_hbm.1) | copy-start | bytes 7864324
  2.4 1.4 %copy-start.1 = (bf16[3,512,512]{2,1,0:T(8,128)(2,1)S(1)}, bf16[3,512,512]{2,1,0:T(8,128)(2,1)}, u32[]{:S(2)}) copy-start(bf16[3,512,512]{2,1,0:T(8,128)(2,1)} %near_hbm.1) | copy-start | bytes 4718596
  3.8 0.9 %copy-start.2 = (bf16[4,64,512]{2,1,0:T(8,128)(2,1)S(1)}, bf16[4,64,512]{2,1,0:T(8,128)(2,1)}, u32[]{:S(2)}) copy-start(bf16[4,64,512]{2,1,0:T(8,128)(2,1)} %hist_ref.1) | copy-start | bytes 786436
  4.7 0.9 %copy-start.3 = (f32[64,512]{1,0:T(8,128)S(1)}, f32[64,512]{1,0:T(8,128)}, u32[]{:S(2)}) copy-start(f32[64,512]{1,0:T(8,128)} %param.15) | copy-start | bytes 393220
  5.6 0.7 %copy-start.4 = (f32[512]{0:T(512)S(1)}, f32[512]{0:T(512)}, u32[]{:S(2)}) copy-start(f32[512]{0:T(512)} %param.14) | copy-start | bytes 6148
  6.3 0.7 %copy-start.5 = (s32[32,1]{0,1:T(1,128)S(1)}, s32[32,1]{0,1:T(1,128)}, u32[]{:S(2)}) copy-start(s32[32,1]{0,1:T(1,128)} %param.12) | copy-start | bytes 388
  7.0 0.7 %copy-start.6 = (s32[32,1]{0,1:T(1,128)S(1)}, s32[32,1]{0,1:T(1,128)}, u32[]{:S(2)}) copy-start(s32[32,1]{0,1:T(1,128)} %param.11) | copy-start | bytes 388

commit v2 on v1

--- a/solution.py
+++ b/solution.py
@@ -23,10 +23,10 @@
 
 def kernel(
     dims,
-    lag_ref, rank_ref, hist_ref, self_ref, exc_ref, right_hbm, left_hbm, near_hbm,
-    cur_out, hist_out,
-    rbuf, lbuf, nbuf, p1, r1, q, r2, t3, r3, xs, halo, xlast, gath, hin,
-    rsem, lsem, nsem, s1s, s1r, s2s, s2r, s3s, s3r, xss, xsr, gs, gr, hs,
+    lag_hbm, rank_hbm, hist_hbm, self_hbm, exc_hbm, right_hbm, left_hbm, near_hbm,
+    cur_hbm, hist_hbm_out,
+    lag_ref, rank_ref, hist_ref, self_ref, exc_ref, cur_out, newest, rbuf, lbuf, nbuf, p1, r1, q, r2, t3, r3, xs, halo, xlast, gath, hin,
+    rsem, lsem, nsem, s1s, s1r, s2s, s2r, s3s, s3r, xss, xsr, gs, gr, hs, isem, osem,
 ):
     space, hists, z_size, x_size, per, rank_most = dims
     lags, steps, width = hist_ref.shape
@@ -58,6 +58,19 @@
     def space_id(zt, xt):
         return (zt * x_size + xt) * 2 + core
 
+    inputs = [
+        pltpu.make_async_copy(a, b, isem.at[i])
+        for i, (a, b) in enumerate((
+            (hist_hbm, hist_ref), (lag_hbm, lag_ref), (rank_hbm, rank_ref),
+            (exc_hbm.at[h], exc_ref), (self_hbm, self_ref),
+        ))
+    ]
+    shift = pltpu.make_async_copy(
+        hist_hbm.at[pl.ds(0, lags - 1)], hist_hbm_out.at[pl.ds(1, lags - 1)], osem.at[2]
+    )
+    for c in inputs[:3]:
+        c.start()
+
     barrier = pltpu.get_barrier_semaphore()
 
     def greet(s, hh):
@@ -89,7 +102,12 @@
         lax.fori_loop(0, half, start, 0)
     near_copy = pltpu.make_async_copy(near_hbm, nbuf, nsem)
     near_copy.start()
-
+    inputs[3].start()
+    inputs[4].start()
+    shift.start()
+
+    for c in inputs[:3]:
+        c.wait()
     hist_all = hist_ref[...].reshape(lags * steps, width)
     cols = lax.broadcasted_iota(jnp.int32, (1, per * rank_most), 1)
 
@@ -194,9 +212,9 @@
     lax.fori_loop(0, z_size - 1, third, 0)
     far = gather2(z)
 
+    inputs[3].wait()
+    inputs[4].wait()
     inverse = 1.0 / self_ref[...]
-    for l in range(1, lags):
-        hist_out[l] = hist_ref[l - 1]
 
     @pl.when(me == 0)
     def _():
@@ -216,7 +234,7 @@
         ).wait_recv()
         far = far + r3[zs].astype(jnp.float32)
     near_copy.wait()
-    right_side = exc_ref[h] - far
+    right_side = exc_ref[...] - far
     current = right_side * inverse
 
     def edge(n, side):
@@ -298,16 +316,24 @@
             device_id=(me, hs_), device_id_type=MESH,
         ).wait_recv()
         cur_out[hs_] = gath[hs_]
+    out_cur = pltpu.make_async_copy(cur_out, cur_hbm, osem.at[0])
+    out_cur.start()
     for o in range(1, hists):
         give(o).wait_send()
 
     @pl.when(h == 0)
     def _():
-        hist_out[0] = cur_out[...].reshape(steps, width).astype(jnp.bfloat16)
+        newest[...] = cur_out[...].reshape(steps, width).astype(jnp.bfloat16)
 
     @pl.when(h > 0)
     def _():
-        hist_out[0] = hin[...]
+        newest[...] = hin[...]
+
+    out_hist = pltpu.make_async_copy(newest, hist_hbm_out.at[0], osem.at[1])
+    out_hist.start()
+    shift.wait()
+    out_cur.wait()
+    out_hist.wait()
 
 
 def per_device(
@@ -323,9 +349,7 @@
     sweeps = SWEEPS - 1
     bf16 = jnp.bfloat16
     dma = pltpu.SemaphoreType.DMA
-    vmem = pl.BlockSpec(memory_space=pltpu.VMEM)
-    smem = pl.BlockSpec(memory_space=pltpu.SMEM)
-    any_ = pl.BlockSpec(memory_space=pl.ANY)
+    hbm = pl.BlockSpec(memory_space=pltpu.HBM)
     flops = 2 * pair_dev * rank_most * width * steps * 2
     current, next_history = pl.pallas_call(
         functools.partial(kernel, (space, hists, z_size, x_size, per, rank_most)),
@@ -333,9 +357,16 @@
             jax.ShapeDtypeStruct((hists, kh, width), jnp.float32),
             jax.ShapeDtypeStruct((lags, steps, width), bf16),
         ),
-        in_specs=[smem, smem, vmem, vmem, vmem, any_, any_, any_],
-        out_specs=(vmem, vmem),
+        in_specs=[hbm] * 8,
+        out_specs=(hbm, hbm),
         scratch_shapes=[
+            pltpu.SMEM((pair_dev,), jnp.int32),
+            pltpu.SMEM((pair_dev,), jnp.int32),
+            pltpu.VMEM((lags, steps, width), bf16),
+            pltpu.VMEM((1, width), jnp.float32),
+            pltpu.VMEM((kh, width), jnp.float32),
+            pltpu.VMEM((hists, kh, width), jnp.float32),
+            pltpu.VMEM((steps, width), bf16),
             pltpu.VMEM((pair_dev, rank_most, width), bf16),
             pltpu.VMEM((pair_dev, rank_most, width), bf16),
             pltpu.VMEM(near_block.shape, bf16),
@@ -355,10 +386,10 @@
             dma((z_size, group)), dma((z_size, group)),
             dma((z_size,)), dma((z_size,)),
             dma((sweeps, 2)), dma((sweeps, 2)),
-            dma((hists,)), dma((hists,)), dma((2,)),
+            dma((hists,)), dma((hists,)), dma((2,)), dma((5,)), dma((3,)),
         ],
         compiler_params=pltpu.CompilerParams(
-            collective_id=0, has_side_effects=True, vmem_limit_bytes=48 * 1024 * 1024
+            collective_id=0, has_side_effects=True, vmem_limit_bytes=64000 * 1024
         ),
         cost_estimate=pl.CostEstimate(
             flops=flops, bytes_accessed=4 * pair_dev * rank_most * width, transcendentals=0

time: 56.2 us -> 49.7 us (0.88)
  local copies, waits for them, and re-layouts: 8.34 us -> 3.24 us
  Pallas kernels: 47 us -> 45.6 us
    unnamed x16 -> x2, local copies, waits for them, and re-layouts: 8.34 us -> 3.24 us
    pallas_call x1, Pallas kernels: 47 us -> 45.6 us  [per_device(): pl.pallas_call(functools.partial(kernel, (space, hists, z_size, x_size, p...]
where the time goes in v2:
time: 49.7 us; the launch traced here: 49.5 us
  Pallas kernels  45.6 us (92%)
  local copies, waits for them, and re-layouts  3.24 us (7%)
  between operations  0.64 us (1%)
    pallas_call x1, Pallas kernels, per_device(): pl.pallas_call(functools.partial(kernel, (space, hists, z_size, x_size, p...  45.6 us
    unnamed x2, local copies, waits for them, and re-layouts  3.24 us

profile of v2, /device:TPU:11, one launch (start us, length us, event | category | flops | bytes accessed | tf_op | source)
XLA Modules:
  0.0 49.5 jit_solution(12208673251731704368)
XLA Ops:
  0.6 45.6 %shard_map.95 = (f32[2,32,512]{2,1,0:T(8,128)}, bf16[4,64,512]{2,1,0:T(8,128)(2,1)}) custom-call(s32[32]{0:T(128)} %bitcast.8, s32[32]{0:T(128)} %bitcast.9, bf16[4,64,512]{2,1,0:T(8,128)(2,1)} %hist_hbm.1, f32[1,512]{1,0:T(1,128)} %bitcast.7, f32[2,32,512]{2,1,0:T(8,128)} %bitcast.5, bf16[32,80,512]{2,1,0:T(8,128)(2,1)} %right_hbm.1, ...), custom_call_target="tpu_custom_call" | custom-call | flops 335544320 | bytes 5242880 | tf_op jit(solution)/shard_map/pallas_call | solution.py:354
  46.3 1.6 %copy.12 = f32[64,512]{1,0:T(8,128)} copy(f32[64,512]{1,0:T(8,128)} %bitcast.6) | data formatting | bytes 262144
  47.8 1.7 %copy.13 = bf16[4,64,512]{2,1,0:T(8,128)(2,1)} copy(bf16[4,64,512]{2,1,0:T(8,128)(2,1)} %get-tuple-element.9) | data formatting | bytes 524288

commit v3 on v2

--- a/solution.py
+++ b/solution.py
@@ -24,13 +24,14 @@
 def kernel(
     dims,
     lag_hbm, rank_hbm, hist_hbm, self_hbm, exc_hbm, right_hbm, left_hbm, near_hbm,
-    cur_hbm, hist_hbm_out,
+    cur_hbm, newest_hbm,
     lag_ref, rank_ref, hist_ref, self_ref, exc_ref, cur_out, newest, rbuf, lbuf, nbuf, p1, r1, q, r2, t3, r3, xs, halo, xlast, gath, hin,
     rsem, lsem, nsem, s1s, s1r, s2s, s2r, s3s, s3r, xss, xsr, gs, gr, hs, isem, osem,
 ):
     space, hists, z_size, x_size, per, rank_most = dims
     lags, steps, width = hist_ref.shape
     kh = steps // hists
+    parts, kg = xlast.shape[0], xlast.shape[1]
     me = lax.axis_index("space")
     h = lax.axis_index("hist")
     core = lax.rem(me, 2)
@@ -65,9 +66,6 @@
             (exc_hbm.at[h], exc_ref), (self_hbm, self_ref),
         ))
     ]
-    shift = pltpu.make_async_copy(
-        hist_hbm.at[pl.ds(0, lags - 1)], hist_hbm_out.at[pl.ds(1, lags - 1)], osem.at[2]
-    )
     for c in inputs[:3]:
         c.start()
 
@@ -104,7 +102,6 @@
     near_copy.start()
     inputs[3].start()
     inputs[4].start()
-    shift.start()
 
     for c in inputs[:3]:
         c.wait()
@@ -219,12 +216,12 @@
     @pl.when(me == 0)
     def _():
         for n in range(SWEEPS - 1):
-            halo[n, 0] = jnp.zeros((kh, width), jnp.bfloat16)
+            halo[n, 0] = jnp.zeros((parts, kg, width), jnp.bfloat16)
 
     @pl.when(me == space - 1)
     def _():
         for n in range(SWEEPS - 1):
-            halo[n, 1] = jnp.zeros((kh, width), jnp.bfloat16)
+            halo[n, 1] = jnp.zeros((parts, kg, width), jnp.bfloat16)
 
     for o in range(1, z_size):
         zs = lax.rem(z + o, z_size)
@@ -235,55 +232,68 @@
         far = far + r3[zs].astype(jnp.float32)
     near_copy.wait()
     right_side = exc_ref[...] - far
-    current = right_side * inverse
-
-    def edge(n, side):
+    right_part = [right_side[g * kg : (g + 1) * kg] for g in range(parts)]
+    current = [r * inverse for r in right_part]
+    rest = [None] * parts
+
+    def edge(n, g, side):
         other = jnp.minimum(me + 1, space - 1) if side == 0 else jnp.maximum(me - 1, 0)
+        i = n * parts + g
         return pltpu.make_async_remote_copy(
-            src_ref=xs.at[n], dst_ref=halo.at[n, side],
-            send_sem=xss.at[n, side], recv_sem=xsr.at[n, side],
+            src_ref=xs.at[n, g], dst_ref=halo.at[n, side, g],
+            send_sem=xss.at[i, side], recv_sem=xsr.at[i, side],
             device_id=(other, h), device_id_type=MESH,
         )
 
-    for n in range(SWEEPS - 1):
-        rounded = current.astype(jnp.bfloat16)
-        xs[n] = rounded
+    def begin(n, g):
+        rounded = current[g].astype(jnp.bfloat16)
+        xs[n, g] = rounded
 
         @pl.when(me < space - 1)
         def _():
-            edge(n, 0).start()
+            edge(n, g, 0).start()
 
         @pl.when(me > 0)
         def _():
-            edge(n, 1).start()
+            edge(n, g, 1).start()
 
         product = lax.dot_general(rounded, nbuf[1], NT, preferred_element_type=jnp.float32)
-        rest = right_side - product
-
-        @pl.when(me > 0)
-        def _():
-            edge(n, 0).wait_recv()
-
-        @pl.when(me < space - 1)
-        def _():
-            edge(n, 1).wait_recv()
-
-        before = lax.dot_general(halo[n, 0], nbuf[0], NT, preferred_element_type=jnp.float32)
-        after = lax.dot_general(halo[n, 1], nbuf[2], NT, preferred_element_type=jnp.float32)
-        current = (rest - before - after) * inverse
-
-    xlast[...] = current
-
-    def give(o):
+        rest[g] = right_part[g] - product
+
+    def give(o, g):
         ht = lax.rem(h + o, hists)
         return pltpu.make_async_remote_copy(
-            src_ref=xlast, dst_ref=gath.at[h], send_sem=gs.at[ht], recv_sem=gr.at[h],
+            src_ref=xlast.at[g], dst_ref=gath.at[h, g],
+            send_sem=gs.at[g, ht], recv_sem=gr.at[g, h],
             device_id=(me, ht), device_id_type=MESH,
         )
 
-    for o in range(1, hists):
-        give(o).start()
-    cur_out[h] = current
+    for g in range(parts):
+        begin(0, g)
+    for n in range(SWEEPS - 1):
+        for g in range(parts):
+            @pl.when(me > 0)
+            def _():
+                edge(n, g, 0).wait_recv()
+
+            @pl.when(me < space - 1)
+            def _():
+                edge(n, g, 1).wait_recv()
+
+            before = lax.dot_general(
+                halo[n, 0, g], nbuf[0], NT, preferred_element_type=jnp.float32
+            )
+            after = lax.dot_general(
+                halo[n, 1, g], nbuf[2], NT, preferred_element_type=jnp.float32
+            )
+            current[g] = (rest[g] - before - after) * inverse
+            if n < SWEEPS - 2:
+                begin(n + 1, g)
+            else:
+                xlast[g] = current[g].astype(jnp.bfloat16)
+                for o in range(1, hists):
+                    give(o, g).start()
+                cur_out[h, g] = current[g]
     hist_copy.wait()
 
     def drain(j, carry):
@@ -302,24 +312,29 @@
     @pl.when(me < space - 1)
     def _():
         for n in range(SWEEPS - 1):
-            edge(n, 0).wait_send()
+            for g in range(parts):
+                edge(n, g, 0).wait_send()
 
     @pl.when(me > 0)
     def _():
         for n in range(SWEEPS - 1):
-            edge(n, 1).wait_send()
-
-    for o in range(1, hists):
-        hs_ = lax.rem(h + o, hists)
-        pltpu.make_async_remote_copy(
-            src_ref=xlast, dst_ref=gath.at[hs_], send_sem=gs.at[hs_], recv_sem=gr.at[hs_],
-            device_id=(me, hs_), device_id_type=MESH,
-        ).wait_recv()
-        cur_out[hs_] = gath[hs_]
+            for g in range(parts):
+                edge(n, g, 1).wait_send()
+
+    for g in range(parts):
+        for o in range(1, hists):
+            hs_ = lax.rem(h + o, hists)
+            pltpu.make_async_remote_copy(
+                src_ref=xlast.at[g], dst_ref=gath.at[hs_, g],
+                send_sem=gs.at[g, hs_], recv_sem=gr.at[g, hs_],
+                device_id=(me, hs_), device_id_type=MESH,
+            ).wait_recv()
+            cur_out[hs_, g] = gath[hs_, g].astype(jnp.float32)
     out_cur = pltpu.make_async_copy(cur_out, cur_hbm, osem.at[0])
     out_cur.start()
     for o in range(1, hists):
-        give(o).wait_send()
+        for g in range(parts):
+            give(o, g).wait_send()
 
     @pl.when(h == 0)
     def _():
@@ -329,11 +344,32 @@
     def _():
         newest[...] = hin[...]
 
-    out_hist = pltpu.make_async_copy(newest, hist_hbm_out.at[0], osem.at[1])
+    out_hist = pltpu.make_async_copy(newest, newest_hbm, osem.at[1])
     out_hist.start()
-    shift.wait()
     out_cur.wait()
     out_hist.wait()
+
+
+def finish(current, newest, history, current_out, history_out, cbuf, hbuf, isem, osem):
+    lags = history.shape[0]
+    older = pl.ds(1, lags - 1)
+    come = [
+        pltpu.make_async_copy(current, cbuf, isem.at[0]),
+        pltpu.make_async_copy(newest, hbuf.at[0], isem.at[1]),
+        pltpu.make_async_copy(history.at[pl.ds(0, lags - 1)], hbuf.at[older], isem.at[2]),
+    ]
+    go = [
+        pltpu.make_async_copy(cbuf, current_out, osem.at[0]),
+        pltpu.make_async_copy(hbuf.at[0], history_out.at[0], osem.at[1]),
+        pltpu.make_async_copy(hbuf.at[older], history_out.at[older], osem.at[2]),
+    ]
+    for c in come:
+        c.start()
+    for c, d in zip(come, go):
+        c.wait()
+        d.start()
+    for d in go:
+        d.wait()
 
 
 def per_device(
@@ -345,17 +381,19 @@
     z_size, x_size, _ = shape_of(space)
     per = pair_dev // space
     kh = steps // hists
+    parts = 2 if kh % 32 == 0 else 1
+    kg = kh // parts
     half, group = space // 2, x_size * hists
     sweeps = SWEEPS - 1
     bf16 = jnp.bfloat16
     dma = pltpu.SemaphoreType.DMA
     hbm = pl.BlockSpec(memory_space=pltpu.HBM)
     flops = 2 * pair_dev * rank_most * width * steps * 2
-    current, next_history = pl.pallas_call(
+    current, newest = pl.pallas_call(
         functools.partial(kernel, (space, hists, z_size, x_size, per, rank_most)),
         out_shape=(
-            jax.ShapeDtypeStruct((hists, kh, width), jnp.float32),
-            jax.ShapeDtypeStruct((lags, steps, width), bf16),
+            jax.ShapeDtypeStruct((hists, parts, kg, width), jnp.float32),
+            jax.ShapeDtypeStruct((steps, width), bf16),
         ),
         in_specs=[hbm] * 8,
         out_specs=(hbm, hbm),
@@ -365,7 +403,7 @@
             pltpu.VMEM((lags, steps, width), bf16),
             pltpu.VMEM((1, width), jnp.float32),
             pltpu.VMEM((kh, width), jnp.float32),
-            pltpu.VMEM((hists, kh, width), jnp.float32),
+            pltpu.VMEM((hists, parts, kg, width), jnp.float32),
             pltpu.VMEM((steps, width), bf16),
             pltpu.VMEM((pair_dev, rank_most, width), bf16),
             pltpu.VMEM((pair_dev, rank_most, width), bf16),
@@ -376,17 +414,17 @@
             pltpu.VMEM((z_size, group, kh, width), bf16),
             pltpu.VMEM((z_size, kh, width), bf16),
             pltpu.VMEM((z_size, kh, width), bf16),
-            pltpu.VMEM((sweeps, kh, width), bf16),
-            pltpu.VMEM((sweeps, 2, kh, width), bf16),
-            pltpu.VMEM((kh, width), jnp.float32),
-            pltpu.VMEM((hists, kh, width), jnp.float32),
+            pltpu.VMEM((sweeps, parts, kg, width), bf16),
+            pltpu.VMEM((sweeps, 2, parts, kg, width), bf16),
+            pltpu.VMEM((parts, kg, width), bf16),
+            pltpu.VMEM((hists, parts, kg, width), bf16),
             pltpu.VMEM((steps, width), bf16),
             dma((space,)), dma((space,)), dma,
             dma((half,)), dma((half,)),
             dma((z_size, group)), dma((z_size, group)),
             dma((z_size,)), dma((z_size,)),
-            dma((sweeps, 2)), dma((sweeps, 2)),
-            dma((hists,)), dma((hists,)), dma((2,)), dma((5,)), dma((3,)),
+            dma((sweeps * parts, 2)), dma((sweeps * parts, 2)),
+            dma((parts, hists)), dma((parts, hists)), dma((2,)), dma((5,)), dma((2,)),
         ],
         compiler_params=pltpu.CompilerParams(
             collective_id=0, has_side_effects=True, vmem_limit_bytes=64000 * 1024
@@ -398,7 +436,21 @@
         pair_lag.reshape(-1), pair_rank.reshape(-1), history, self_term.reshape(1, width),
         excitation.reshape(hists, kh, width), right_factor, left_factor, near_block,
     )
-    return current.reshape(steps, width), next_history
+    return pl.pallas_call(
+        finish,
+        out_shape=(
+            jax.ShapeDtypeStruct((steps, width), jnp.float32),
+            jax.ShapeDtypeStruct((lags, steps, width), bf16),
+        ),
+        in_specs=[hbm] * 3,
+        out_specs=(hbm, hbm),
+        scratch_shapes=[
+            pltpu.VMEM((steps, width), jnp.float32),
+            pltpu.VMEM((lags, steps, width), bf16),
+            dma((3,)), dma((3,)),
+        ],
+        compiler_params=pltpu.CompilerParams(vmem_limit_bytes=64000 * 1024),
+    )(current.reshape(steps, width), newest, history)
 
 
 def solution(mesh):

time: 49.7 us -> 47.2 us (0.950)
  local copies, waits for them, and re-layouts: 3.24 us -> 0 us
  Pallas kernels: 45.6 us -> 46.4 us
    unnamed x2 -> x0, local copies, waits for them, and re-layouts: 3.24 us -> none
    pallas_call x0 -> x1, Pallas kernels: none -> 1.75 us  [per_device(): pl.pallas_call(finish, out_shape=(jax.ShapeDtypeStruct((steps, width), jn...]
    pallas_call x1, Pallas kernels: 45.6 us -> 44.6 us  [per_device(): pl.pallas_call(functools.partial(kernel, (space, hists, z_size, x_size, p...]
where the time goes in v3:
time: 47.2 us; the launch traced here: 47 us
  Pallas kernels  46.4 us (98%)
  between operations  0.64 us (1%)
    pallas_call x1, Pallas kernels, per_device(): pl.pallas_call(functools.partial(kernel, (space, hists, z_size, x_size, p...  44.6 us
    pallas_call x1, Pallas kernels, per_device(): pl.pallas_call(finish, out_shape=(jax.ShapeDtypeStruct((steps, width), jn...  1.75 us

profile of v3, /device:TPU:11, one launch (start us, length us, event | category | flops | bytes accessed | tf_op | source)
XLA Modules:
  0.0 47.0 jit_solution(9830699184996521650)
XLA Ops:
  0.6 44.6 %shard_map.95 = (f32[2,2,16,512]{3,2,1,0:T(8,128)}, bf16[64,512]{1,0:T(8,128)(2,1)}) custom-call(s32[32]{0:T(128)} %bitcast.8, s32[32]{0:T(128)} %bitcast.9, bf16[4,64,512]{2,1,0:T(8,128)(2,1)} %history.1, f32[1,512]{1,0:T(1,128)} %bitcast.7, f32[2,32,512]{2,1,0:T(8,128)} %bitcast.5, bf16[32,80,512]{2,1,0:T(8,128)(2,1)} %right_hbm.1, ...), custom_call_target="tpu_custom_call" | custom-call | flops 335544320 | bytes 5242880 | tf_op jit(solution)/shard_map/pallas_call | solution.py:392
  45.3 1.8 %shard_map.96 = (f32[64,512]{1,0:T(8,128)}, bf16[4,64,512]{2,1,0:T(8,128)(2,1)}) custom-call(f32[64,512]{1,0:T(8,128)} %bitcast.6, bf16[64,512]{1,0:T(8,128)(2,1)} %get-tuple-element.5.newest, bf16[4,64,512]{2,1,0:T(8,128)(2,1)} %history.1), custom_call_target="tpu_custom_call" | custom-call | tf_op jit(solution)/shard_map/pallas_call | solution.py:439
